TPU v7x, 256 devices: a whole 4x4x8 slice. The times are simulated.
256 devices in a mesh: dom: 32 (over y, z_hi, core), rep: 8 (over x, z_lo).
Axes of the slice: x: 4, y: 4, z: 8 (z_hi: 4, z_lo: 2; z = z_hi * 2 + z_lo), core: 2. Of those that a mesh axis runs over, the one named last changes fastest.
Arguments:
- features: bfloat16 [16384, 768], P('dom'), may hold values from -6 to 6
- tiles: bfloat16 [128, 32, 4, 128, 128], P('dom', 'rep'), may hold values from -0.046875 to 0.046875
- tile_cols: int32 [128, 32, 4], P('dom', 'rep'), may hold values from 0 to 3
- tile_mask: int32 [128, 32, 4], P('dom', 'rep'), may hold values from 0 to 1, as said below
- weight: bfloat16 [768, 768], replicated, may hold values from -0.21875 to 0.21875
- bias: float32 [768], replicated, may hold values from -3 to 3
- cotangent: bfloat16 [16384, 768], P(('dom', 'rep')), may hold values from -0.046875 to 0.046875
Outputs:
- output: bfloat16 [16384, 768], P(('dom', 'rep'))
- grad_weight: float32 [768, 768], replicated
- grad_bias: float32 [768], replicated
Inputs may be any that keep to these rules, and one draw needn't show every extreme that they name: `tile_mask`: for each row block and source, the live slots come first and slot 0 is always live.
All inputs are finite; a program needn't handle non-finite values.
Results may differ from a plain program's by a relative error of at most 0.02.
Values may be sent and summed in bfloat16 or wider, within the bound.
No kernel may reach another device: no remote copies, remote signals or barrier semaphores. Data moves between devices by JAX's collectives and lax.ppermute only.
A program may use at most 128 MiB of HBM per device.

v0:
```python
import jax
import jax.numpy as jnp
from jax import lax
from jax.sharding import PartitionSpec as P


def spread(value, axis, source):
    kept = jnp.where(lax.axis_index(axis) == source, value, 0).astype(value.dtype)
    return lax.psum(kept, axis)


def section_term(source, tiles, tile_cols, tile_mask, section):
    rblocks = tiles.shape[0]
    tile_side = tiles.shape[3]
    feat_width = source.shape[1]
    source_blocks = source.reshape(source.shape[0] // tile_side, tile_side, feat_width)
    columns = lax.dynamic_index_in_dim(tile_cols, section, 1, keepdims=False)
    live = lax.dynamic_index_in_dim(tile_mask, section, 1, keepdims=False)
    tile_set = lax.dynamic_index_in_dim(tiles, section, 1, keepdims=False)
    block_ids = jnp.arange(source_blocks.shape[0])
    selector = ((columns[:, :, None] == block_ids[None, None, :]) * live[:, :, None]).astype(
        jnp.bfloat16
    )
    picked = jnp.einsum(
        "bkc,cjd->bkjd", selector, source_blocks, preferred_element_type=jnp.float32
    ).astype(jnp.bfloat16)
    summed = jnp.einsum("bkij,bkjd->bid", tile_set, picked, preferred_element_type=jnp.float32)
    return summed.reshape(rblocks * tile_side, feat_width)


def on_device(features, tiles, tile_cols, tile_mask, weight, bias, cotangent):
    sections = tiles.shape[1]
    replica = lax.axis_index("rep")
    aggregate = jnp.zeros(features.shape, jnp.float32)
    for turn_index in range(sections):
        root_index = replica * sections + turn_index
        source = spread(features, "dom", root_index)
        aggregate = aggregate + section_term(source, tiles, tile_cols, tile_mask, turn_index)
    rows_sum = lax.psum_scatter(
        aggregate.astype(jnp.bfloat16), "rep", scatter_dimension=0, tiled=True
    )
    pre_act = jnp.dot(rows_sum, weight, preferred_element_type=jnp.float32) + bias
    sigmoid_pre = jax.nn.sigmoid(pre_act)
    output = (pre_act * sigmoid_pre).astype(jnp.bfloat16)
    grad_pre = cotangent.astype(jnp.float32) * sigmoid_pre * (1.0 + pre_act * (1.0 - sigmoid_pre))
    grad_low = grad_pre.astype(jnp.bfloat16)
    local_weight = jnp.einsum("nd,ne->de", rows_sum, grad_low, preferred_element_type=jnp.float32)
    local_bias = jnp.sum(grad_pre, axis=0)
    grad_weight, grad_bias = lax.psum((local_weight, local_bias), ("dom", "rep"))
    return (output, grad_weight, grad_bias)


def solution(mesh):
    placed = (
        P("dom", None),
        P("dom", "rep", None, None, None),
        P("dom", "rep", None),
        P("dom", "rep", None),
        P(),
        P(),
        P(("dom", "rep"), None),
    )
    return jax.shard_map(
        on_device,
        mesh=mesh,
        in_specs=placed,
        out_specs=(P(("dom", "rep"), None), P(), P()),
        check_vma=False,
    )
```

profile of v0, /device:TPU:2, one launch (start us, length us, event | category | flops | bytes accessed | tf_op | source)
XLA Modules:
  0.0 638.1 jit_solution(3435864758097265437)
XLA Ops:
  7.2 0.0 copy-start
  7.2 0.0 all-reduce.6.cloned.1.call-start
  7.2 3.0 broadcast_select_fusion
  10.2 0.0 copy-start.6
  10.2 0.0 copy-start.7
  10.2 0.0 all-reduce.6.cloned.1.call-update
  10.2 0.0 copy-start.1
  10.3 0.0 reduce-scatter.2.cloned.1.call-start
  10.3 0.6 copy-done.6
  10.9 0.0 copy-done.7
  10.9 298.5 %all-reduce.6.cloned.1.call-done = (bf16[4,128,768]{2,1,0:T(8,128)(2,1)}, bf16[4,128,768]{2,1,0:T(8,128)(2,1)}, bf16[4,128,768]{2,1,0:T(8,128)(2,1)}, bf16[4,128,768]{2,1,0:T(8,128)(2,1)}) async-done(((bf16[4,128,768]{2,1,0:T(8,128)(2,1)}, bf16[4,128,768]{2,1,0:T(8,128)(2,1)}, bf16[4,128,768]{2,1,0:T(8,128)(2,1)}, bf16[4,128,768]{2,1,0:T(8,128)(2,1)}), (bf16[4,128,768]{2,1,0:T(8,128)(2,1)}, ...) | async-done | bytes 3145744 | tf_op jit(solution)/shard_map/psum | solution.py:9
  309.4 2.5 fusion.9
  312.0 0.0 copy-done.1
  312.0 0.0 copy-start.4
  312.0 0.6 fusion.1
  312.6 0.5 copy-done.4
  313.1 1.4 fusion.7
  314.5 0.0 copy-start.3
  314.5 0.6 fusion.2
  315.1 0.5 copy-done.3
  315.6 1.4 fusion.11
  317.0 0.0 copy-start.2
  317.0 0.6 fusion
  317.6 0.5 copy-done.2
  318.1 1.4 fusion.5
  319.5 0.0 copy-start.5
  319.5 0.0 copy-start.8
  319.5 1.8 fusion.4
  321.3 0.0 reduce-scatter.2.cloned.1.call-update
  321.3 0.0 all-reduce.4.cloned.1.call-start
  321.4 38.8 %reduce-scatter.2.cloned.1.call-done = bf16[64,768]{1,0:T(8,128)(2,1)} async-done(((bf16[512,768]{1,0:T(8,128)(2,1)}), bf16[64,768]{1,0:T(8,128)(2,1)}) %reduce-scatter.2.cloned.1.call-update) | async-done | bytes 98320 | tf_op jit(solution)/shard_map/reduce_scatter | solution.py:39
  360.2 0.0 copy-done
  360.2 0.0 copy-done.5
  360.2 0.0 copy-done.8
  360.2 1.9 fusion.47
  362.1 2.8 fusion.21
  364.9 0.0 all-reduce.4.cloned.1.call-update
  364.9 75.7 %psum.47 = f32[768]{0:T(1024)} all-reduce(f32[768]{0:T(1024)S(1)} %get-tuple-element.11), channel_id=1, replica_groups=mesh['dom'=32,'rep'=8] {'dom','rep'}, use_global_device_ids=true, to_apply=%region_7.8 | all-reduce | flops 768 | bytes 6144 | tf_op jit(solution)/shard_map/psum | solution.py:49
  440.6 187.7 %all-reduce.4.cloned.1.call-done = f32[768,768]{1,0:T(8,128)} async-done(((f32[768,768]{1,0:T(8,128)}), f32[768,768]{1,0:T(8,128)}) %all-reduce.4.cloned.1.call-update) | async-done | bytes 2359312 | tf_op jit(solution)/shard_map/psum | solution.py:49
  628.3 3.2 copy.57
  (2 shorter events, 0.0 us)
Async XLA Ops:
  7.2 353.0 %copy-start = (bf16[768,768]{1,0:T(8,128)(2,1)S(1)}, bf16[768,768]{1,0:T(8,128)(2,1)}, u32[]{:S(2)}) copy-start(bf16[768,768]{1,0:T(8,128)(2,1)} %param.11) | copy-start | bytes 3538948
  7.2 302.3 %all-reduce.6.cloned.1.call-start = ((), (), s32[]{:S(2)}) async-start(), calls=%async_computation.3 | async-start | bytes 6291456 | tf_op jit(solution)/shard_map/psum | solution.py:9
  10.2 0.7 copy-start.6
  10.2 0.7 copy-start.7
  10.2 301.7 %copy-start.1 = (bf16[4,4,4,128,128]{4,3,2,1,0:T(8,128)(2,1)S(1)}, bf16[4,4,4,128,128]{4,3,2,1,0:T(8,128)(2,1)}, u32[]{:S(2)}) copy-start(bf16[4,4,4,128,128]{4,3,2,1,0:T(8,128)(2,1)} %param.8) | copy-start | bytes 6291460
  10.3 349.9 %reduce-scatter.2.cloned.1.call-start = ((), (), s32[]{:S(2)}) async-start(), calls=%async_computation.1 | async-start | bytes 884736 | tf_op jit(solution)/shard_map/reduce_scatter | solution.py:39
  312.0 1.1 copy-start.4
  314.5 1.1 copy-start.3
  317.0 1.1 copy-start.2
  319.5 40.7 %copy-start.5 = (bf16[64,768]{1,0:T(8,128)(2,1)S(1)}, bf16[64,768]{1,0:T(8,128)(2,1)}, u32[]{:S(2)}) copy-start(bf16[64,768]{1,0:T(8,128)(2,1)} %param.13) | copy-start | bytes 294916
  319.5 40.7 %copy-start.8 = (f32[768]{0:T(1024)S(1)}, f32[768]{0:T(1024)}, u32[]{:S(2)}) copy-start(f32[768]{0:T(1024)} %param.12) | copy-start | bytes 9220
  321.3 307.0 %all-reduce.4.cloned.1.call-start = ((), (), s32[]{:S(2)}) async-start(), calls=%async_computation.2 | async-start | bytes 4718592 | tf_op jit(solution)/shard_map/psum | solution.py:49
Sparse Core Ops, SparseCore 0:
  11.5 297.9 all-reduce.5
  321.4 38.6 reduce-scatter.1
  366.2 262.1 all-reduce.3
where the time goes:
time: 639 us; the launch traced here: 638 us
  waiting for transfers between devices  525 us (82%)
  blocking collectives  75.7 us (12%)
  matrix products  14.9 us (2%)
  between operations  13.9 us (2%)
    psum x1, waiting for transfers between devices, spread(): return lax.psum(kept, axis)  299 us
    psum x1, waiting for transfers between devices, on_device(): lax.psum((local_weight, local_bias), ('dom', 'rep'))  188 us
    psum x1, blocking collectives, on_device(): lax.psum((local_weight, local_bias), ('dom', 'rep'))  75.7 us
    reduce_scatter x1, waiting for transfers between devices, on_device(): lax.psum_scatter(aggregate.astype(jnp.bfloat16), 'rep', scatter_dimension...  38.8 us
  transfers between devices with their start and end apart: 3, of which 3 were waited for; matrix products, arithmetic and copies ran while one was open for 0% of the time, Pallas kernels for 0%

commit v1 on v0

--- a/solution.py
+++ b/solution.py
@@ -6,7 +6,7 @@
 
 def spread(value, axis, source):
     kept = jnp.where(lax.axis_index(axis) == source, value, 0).astype(value.dtype)
-    return lax.psum(kept, axis)
+    return jnp.sum(lax.all_gather(kept, axis), axis=0)
 
 
 def section_term(source, tiles, tile_cols, tile_mask, section):

time: 639 us -> 1000 us (1.56)
  waiting for transfers between devices: 525 us -> 838 us
  other arithmetic: 2.97 us -> 56.1 us
    all_gather x0 -> x4, waiting for transfers between devices: none -> 597 us  [spread(): return jnp.sum(lax.all_gather(kept, axis), axis=0)]
    psum x1 -> x0, waiting for transfers between devices: 299 us -> none  [spread(): return lax.psum(kept, axis)]
    reduce_sum x0 -> x4, other arithmetic: none -> 53.2 us  [spread(): return jnp.sum(lax.all_gather(kept, axis), axis=0)]
    reduce_scatter x1, waiting for transfers between devices: 38.8 us -> 50.7 us  [on_device(): lax.psum_scatter(aggregate.astype(jnp.bfloat16), 'rep', scatter_dimension...]
  transfers between devices with their start and end apart: 3 -> 6, of which waited for: 3 -> 6; matrix products, arithmetic and copies ran while one was open for 0% -> 4% of each run, Pallas kernels for 0% -> 0%
where the time goes in v1:
time: 1000 us
  waiting for transfers between devices  838 us (84%)
  blocking collectives  75.7 us (8%)
  other arithmetic  56.1 us (6%)
  matrix products  15.1 us (2%)
  between operations  14.2 us (1%)
    all_gather x4, waiting for transfers between devices, spread(): return jnp.sum(lax.all_gather(kept, axis), axis=0)  597 us
    psum x1, waiting for transfers between devices, on_device(): lax.psum((local_weight, local_bias), ('dom', 'rep'))  188 us
    psum x1, blocking collectives, on_device(): lax.psum((local_weight, local_bias), ('dom', 'rep'))  75.7 us
    reduce_sum x4, other arithmetic, spread(): return jnp.sum(lax.all_gather(kept, axis), axis=0)  53.2 us
    reduce_scatter x1, waiting for transfers between devices, on_device(): lax.psum_scatter(aggregate.astype(jnp.bfloat16), 'rep', scatter_dimension...  50.7 us
  transfers between devices with their start and end apart: 6, of which 6 were waited for; matrix products, arithmetic and copies ran while one was open for 4% of the time, Pallas kernels for 0%

profile of v1, /device:TPU:2, one launch (start us, length us, event | category | flops | bytes accessed | tf_op | source)
XLA Modules:
  0.0 1003.7 jit_solution(3908359622612933550)
XLA Ops:
  7.2 0.0 copy-start
  7.2 0.0 all-gather.15.cloned.1.call-start
  7.2 2.9 broadcast_select_fusion
  10.2 0.0 all-gather.15.cloned.1.call-update
  10.2 0.0 all-gather.11.cloned.1.call-start
  10.2 0.7 all-gather.11.cloned.1.call-update
  11.0 0.0 all-gather.9.cloned.1.call-start
  11.0 0.7 all-gather.9.cloned.1.call-update
  11.7 0.0 all-gather.13.cloned.1.call-start
  11.7 0.5 all-gather.13.cloned.1.call-update
  12.3 0.0 reduce-scatter.2.cloned.1.call-start
  12.3 0.0 copy-done.5
  12.3 0.6 fusion.48
  12.9 0.0 copy-done.6
  12.9 0.6 fusion.49
  13.5 149.7 %all-gather.15.cloned.1.call-done = bf16[16384,768]{1,0:T(8,128)(2,1)} async-done(((bf16[512,768]{1,0:T(8,128)(2,1)}), bf16[16384,768]{1,0:T(8,128)(2,1)}) %all-gather.15.cloned.1.call-update) | async-done | bytes 25165840 | tf_op jit(solution)/shard_map/all_gather | solution.py:9
  163.2 13.1 %reduce_sum.60 = bf16[512,768]{1,0:T(8,128)(2,1)S(1)} reduce(bf16[32,512,768]{2,1,0:T(8,128)(2,1)} %bitcast.88, bf16[]{:T(256)} %constant.59.clone.1), dimensions={0}, to_apply=%region_3.4 | reduce | flops 12189696 | bytes 25952258 | tf_op jit(solution)/shard_map/reduce_sum | solution.py:9
  176.3 149.1 %all-gather.11.cloned.1.call-done = bf16[16384,768]{1,0:T(8,128)(2,1)} async-done(((bf16[512,768]{1,0:T(8,128)(2,1)}), bf16[16384,768]{1,0:T(8,128)(2,1)}) %all-gather.11.cloned.1.call-update) | async-done | bytes 25165840 | tf_op jit(solution)/shard_map/all_gather | solution.py:9
  325.4 13.1 %reduce_sum.58 = bf16[512,768]{1,0:T(8,128)(2,1)S(1)} reduce(bf16[32,512,768]{2,1,0:T(8,128)(2,1)} %bitcast.89, bf16[]{:T(256)} %constant.59.clone.1), dimensions={0}, to_apply=%region_1.2 | reduce | flops 12189696 | bytes 25952258 | tf_op jit(solution)/shard_map/reduce_sum | solution.py:9
  338.5 149.2 %all-gather.9.cloned.1.call-done = bf16[16384,768]{1,0:T(8,128)(2,1)} async-done(((bf16[512,768]{1,0:T(8,128)(2,1)}), bf16[16384,768]{1,0:T(8,128)(2,1)}) %all-gather.9.cloned.1.call-update) | async-done | bytes 25165840 | tf_op jit(solution)/shard_map/all_gather | solution.py:9
  487.7 13.1 %reduce_sum.57 = bf16[512,768]{1,0:T(8,128)(2,1)S(1)} reduce(bf16[32,512,768]{2,1,0:T(8,128)(2,1)} %bitcast.90, bf16[]{:T(256)} %constant.59.clone.1), dimensions={0}, to_apply=%region_0.1 | reduce | flops 12189696 | bytes 25952258 | tf_op jit(solution)/shard_map/reduce_sum | solution.py:9
  500.7 149.0 %all-gather.13.cloned.1.call-done = bf16[16384,768]{1,0:T(8,128)(2,1)} async-done(((bf16[512,768]{1,0:T(8,128)(2,1)}), bf16[16384,768]{1,0:T(8,128)(2,1)}) %all-gather.13.cloned.1.call-update) | async-done | bytes 25165840 | tf_op jit(solution)/shard_map/all_gather | solution.py:9
  649.7 14.0 %reduce_sum.59 = bf16[512,768]{1,0:T(8,128)(2,1)} reduce(bf16[32,512,768]{2,1,0:T(8,128)(2,1)} %bitcast.91, bf16[]{:T(256)} %constant.59.clone.1), dimensions={0}, to_apply=%region_2.3 | reduce | flops 12189696 | bytes 25952258 | tf_op jit(solution)/shard_map/reduce_sum | solution.py:9
  663.7 2.7 fusion.7
  666.3 0.0 copy-done.1
  666.3 0.0 copy-start.3
  666.4 0.0 copy-start.4
  666.4 0.6 fusion.2
  667.0 0.0 copy-done.3
  667.0 0.0 copy-done.4
  667.0 1.4 fusion.11
  668.4 0.6 fusion
  669.0 1.4 fusion.9
  670.4 0.6 fusion.1
  671.0 1.4 fusion.5
  672.4 0.0 copy-start.2
  672.4 0.0 copy-start.7
  672.4 1.8 fusion.4
  674.2 0.0 reduce-scatter.2.cloned.1.call-update
  674.2 0.0 all-reduce.2.cloned.1.call-start
  674.3 50.7 %reduce-scatter.2.cloned.1.call-done = bf16[64,768]{1,0:T(8,128)(2,1)} async-done(((bf16[512,768]{1,0:T(8,128)(2,1)}), bf16[64,768]{1,0:T(8,128)(2,1)}) %reduce-scatter.2.cloned.1.call-update) | async-done | bytes 98320 | tf_op jit(solution)/shard_map/reduce_scatter | solution.py:39
  725.0 0.0 copy-done.2
  725.0 1.9 fusion.47
  726.9 2.8 fusion.21
  729.7 0.0 all-reduce.2.cloned.1.call-update
  729.7 75.7 %psum.15 = f32[768]{0:T(1024)} all-reduce(f32[768]{0:T(1024)S(1)} %get-tuple-element.7), channel_id=1, replica_groups=mesh['dom'=32,'rep'=8] {'dom','rep'}, use_global_device_ids=true, to_apply=%region_7.8 | all-reduce | flops 768 | bytes 6144 | tf_op jit(solution)/shard_map/psum | solution.py:49
  805.4 188.2 %all-reduce.2.cloned.1.call-done = f32[768,768]{1,0:T(8,128)} async-done(((f32[768,768]{1,0:T(8,128)}), f32[768,768]{1,0:T(8,128)}) %all-reduce.2.cloned.1.call-update) | async-done | bytes 2359312 | tf_op jit(solution)/shard_map/psum | solution.py:49
  993.6 3.2 copy.53
  (5 shorter events, 0.0 us)
Async XLA Ops:
  7.2 717.8 %copy-start = (bf16[768,768]{1,0:T(8,128)(2,1)S(1)}, bf16[768,768]{1,0:T(8,128)(2,1)}, u32[]{:S(2)}) copy-start(bf16[768,768]{1,0:T(8,128)(2,1)} %param.11) | copy-start | bytes 3538948
  7.2 156.0 %all-gather.15.cloned.1.call-start = ((), (), s32[]{:S(2)}) async-start(), calls=%async_computation.6 | async-start | bytes 25952256 | tf_op jit(solution)/shard_map/all_gather | solution.py:9
  10.2 2.1 copy-start.5
  10.2 2.8 copy-start.6
  10.2 315.2 %all-gather.11.cloned.1.call-start = ((), (), s32[]{:S(2)}) async-start(), calls=%async_computation.4 | async-start | bytes 25952256 | tf_op jit(solution)/shard_map/all_gather | solution.py:9
  11.0 476.7 %all-gather.9.cloned.1.call-start = ((), (), s32[]{:S(2)}) async-start(), calls=%async_computation.3 | async-start | bytes 25952256 | tf_op jit(solution)/shard_map/all_gather | solution.py:9
  11.7 638.0 %all-gather.13.cloned.1.call-start = ((), (), s32[]{:S(2)}) async-start(), calls=%async_computation.5 | async-start | bytes 25952256 | tf_op jit(solution)/shard_map/all_gather | solution.py:9
  12.3 712.7 %reduce-scatter.2.cloned.1.call-start = ((), (), s32[]{:S(2)}) async-start(), calls=%async_computation.1 | async-start | bytes 884736 | tf_op jit(solution)/shard_map/reduce_scatter | solution.py:39
  663.7 2.7 copy-start.1
  666.3 0.7 copy-start.3
  666.4 0.7 copy-start.4
  672.4 52.6 %copy-start.2 = (bf16[64,768]{1,0:T(8,128)(2,1)S(1)}, bf16[64,768]{1,0:T(8,128)(2,1)}, u32[]{:S(2)}) copy-start(bf16[64,768]{1,0:T(8,128)(2,1)} %param.13) | copy-start | bytes 294916
  672.4 52.6 %copy-start.7 = (f32[768]{0:T(1024)S(1)}, f32[768]{0:T(1024)}, u32[]{:S(2)}) copy-start(f32[768]{0:T(1024)} %param.12) | copy-start | bytes 9220
  674.2 319.4 %all-reduce.2.cloned.1.call-start = ((), (), s32[]{:S(2)}) async-start(), calls=%async_computation.2 | async-start | bytes 4718592 | tf_op jit(solution)/shard_map/psum | solution.py:49
Sparse Core Ops, SparseCore 0:
  11.1 152.0 all-gather.14
  165.7 159.6 all-gather.10
  327.9 159.6 all-gather.8
  490.1 159.6 all-gather.12
  674.4 50.5 reduce-scatter.1
  731.7 261.8 all-reduce.1
